TPU v7x, 128 devices: a whole 4x4x4 slice. The times are simulated.
128 devices in a mesh: box: 16 (over y, x), pair: 8 (over z, core).
Axes of the slice: x: 4, y: 4, z: 4, core: 2. Of those that a mesh axis runs over, the one named last changes fastest.
Arguments:
- multipoles: bfloat16 [441, 262144], P(None, ('box', 'pair')), may hold values from -0.5 to 0.5
- density: float32 [262144], P(('box', 'pair')), may hold values from -0.6 to 0.6
- pair_centers: float32 [3, 262144], P(None, ('box', 'pair')), may hold values from 0 to 4
- pair_exponent: float32 [262144], P(('box', 'pair')), may hold values from 0.3 to 6
- box_of_pair: int32 [262144], P(('box', 'pair')), may hold values from 0 to 32767, as said below
- near_tiles: int32 [2048, 24], P(('box', 'pair')), may hold values from 0 to 2047, as said below
- near_count: int32 [2048], P(('box', 'pair')), may hold values from 1 to 24, as said below
- m2l_source: int32 [32768, 16], P('box'), may hold values from -1 to 32767, as said below
- coarse_source: int32 [512, 16], P('box'), may hold values from -1 to 511, as said below
- m2m_ops: bfloat16 [8, 441, 441], replicated, may hold values from -0.109375 to 0.109375
- l2l_ops: bfloat16 [8, 441, 441], replicated, may hold values from -0.25 to 0.25
- m2l_ops: bfloat16 [16, 441, 441], replicated, may hold values from -0.25 to 0.25
Outputs:
- coulomb: float32 [262144], P(('box', 'pair'))
Inputs may be any that keep to these rules, and one draw needn't show every extreme that they name: `box_of_pair`: pairs are sorted by leaf box; the i-th run of 2048 pairs has its leaf boxes in leaves i * 256 to i * 256 + 255. `near_tiles`: the source tiles of a tile lie in the tiles of its own box index or of the box index just before or after it. Only the first near_count[u] entries of row u of near_tiles count; some tile has 24 in every draw. `m2l_source`: -1 marks an absent class; a source is never the target and lies in the block of 2048 leaf boxes of the target's box index or of the box index just before or after it. `coarse_source`: -1 marks an absent class; a source is never the target.
All inputs are finite; a program needn't handle non-finite values.
Results may differ from a plain program's by a relative error of at most 0.0027.
Values may be sent and summed in bfloat16 or wider, within the bound.
A program may use at most 128 MiB of HBM per device.

v0:
```python
import math

import jax
import jax.numpy as jnp
from jax import lax
from jax.sharding import PartitionSpec as P

TILE = 128


cutoff = 0.0001
center_value = 2.0 / math.sqrt(math.pi)


def padded(block, sides, width):
    for axis, dim in sides:
        count = lax.axis_size(axis)
        forward = [(i, i + 1) for i in range(count - 1)]
        backward = [(target, source) for source, target in forward]
        low = lax.ppermute(
            lax.slice_in_dim(block, block.shape[dim] - width, None, axis=dim), axis, forward
        )
        high = lax.ppermute(lax.slice_in_dim(block, 0, width, axis=dim), axis, backward)
        block = jnp.concatenate([low, block, high], axis=dim)
    return block


def interact(own_tiles, source_tiles):
    delta_x = own_tiles[0][:, :, None] - source_tiles[0][:, None, :]
    delta_y = own_tiles[1][:, :, None] - source_tiles[1][:, None, :]
    delta_z = own_tiles[2][:, :, None] - source_tiles[2][:, None, :]
    distance = jnp.sqrt(delta_x * delta_x + delta_y * delta_y + delta_z * delta_z)
    target_exp = own_tiles[3][:, :, None]
    source_exp = source_tiles[3][:, None, :]
    reduced = jnp.sqrt(target_exp * source_exp / (target_exp + source_exp))
    argument = reduced * distance
    safe_arg = jnp.where(argument > cutoff, argument, 1.0)
    shape_fn = jnp.where(
        argument > cutoff, jax.scipy.special.erf(safe_arg) / safe_arg, center_value
    )
    return jnp.sum(reduced * shape_fn * source_tiles[4][:, None, :], axis=2)


def gather_sources(table, source, column_of):
    present = source.T >= 0
    columns = column_of(jnp.maximum(source.T, 0))
    picked = jnp.take(table, columns, axis=1)
    return jnp.where(present[None], picked, jnp.zeros((), jnp.bfloat16))


def translate(operators, picked):
    return jnp.einsum("cpq,qct->pt", operators, picked, preferred_element_type=jnp.float32)


def body(
    multipoles,
    density,
    pair_centers,
    pair_exponent,
    box_of_pair,
    near_tiles,
    near_count,
    m2l_source,
    coarse_source,
    m2m_ops,
    l2l_ops,
    m2l_ops,
):
    npairs_axis = lax.axis_size("pair")
    box_index = lax.axis_index("box")
    pair_index = lax.axis_index("pair")
    coeffs = multipoles.shape[0]
    pairs_dev = multipoles.shape[1]
    leaves = m2l_source.shape[0]
    tiles_dev = near_tiles.shape[0]
    share_cols = leaves // npairs_axis
    packed = jnp.concatenate([pair_centers, pair_exponent[None, :], density[None, :]], axis=0)
    rim_data = padded(packed, (("box", 1),), pairs_dev)
    peer_data = lax.all_gather(rim_data, "pair", axis=1, tiled=True)
    local_box = box_of_pair - box_index * leaves - pair_index * share_cols
    onehot_weights = jnp.where(
        local_box[:, None] == jnp.arange(share_cols, dtype=jnp.int32)[None, :],
        density.astype(jnp.bfloat16)[:, None],
        jnp.zeros((), jnp.bfloat16),
    )
    share_moments = jnp.dot(multipoles, onehot_weights, preferred_element_type=jnp.float32).astype(
        jnp.bfloat16
    )
    own_leaf = lax.all_gather(share_moments, "pair", axis=1, tiled=True)
    extended = padded(own_leaf, (("box", 1),), leaves)

    def leaf_column(source):
        return source - (box_index - 1) * leaves

    targets = lax.dynamic_slice_in_dim(m2l_source, pair_index * share_cols, share_cols, 0)

    def climb(values):
        return jnp.einsum(
            "opq,qmo->pm",
            m2m_ops,
            values.reshape(coeffs, -1, 8),
            preferred_element_type=jnp.float32,
        ).astype(jnp.bfloat16)

    def descend(values):
        return jnp.einsum(
            "opq,qm->pmo", l2l_ops, values, preferred_element_type=jnp.float32
        ).reshape(coeffs, -1)

    middle_moments = climb(own_leaf)
    coarse_moments = climb(middle_moments)
    all_coarse = lax.all_gather(coarse_moments, "box", axis=1, tiled=True)
    coarse_locals = translate(
        m2l_ops, gather_sources(all_coarse, coarse_source, lambda source: source)
    ).astype(jnp.bfloat16)
    middle_locals = descend(coarse_locals).astype(jnp.bfloat16)
    leaf_down = descend(middle_locals)
    translated = translate(m2l_ops, gather_sources(extended, targets, leaf_column))
    down_share = lax.dynamic_slice_in_dim(leaf_down, pair_index * share_cols, share_cols, 1)
    locals_share = (down_share + translated).astype(jnp.bfloat16)
    picked_locals = jnp.take(locals_share, local_box, axis=1)
    far_field = jnp.einsum(
        "kp,kp->p", multipoles, picked_locals, preferred_element_type=jnp.float32
    )
    group_tiles = npairs_axis * tiles_dev
    source_tiles = peer_data.reshape(5, npairs_axis * 3 * tiles_dev, TILE)
    own_tiles = packed.reshape(5, tiles_dev, TILE)

    def tile_slot(global_tile):
        block_offset = global_tile // group_tiles - box_index + 1
        within_block = global_tile % group_tiles
        return (
            within_block // tiles_dev * (3 * tiles_dev)
            + block_offset * tiles_dev
            + within_block % tiles_dev
        )

    def near_step(column, totals):
        wanted = lax.dynamic_index_in_dim(near_tiles, column, 1, keepdims=False)
        fetched = jnp.take(source_tiles, tile_slot(wanted), axis=1)
        contrib = interact(own_tiles, fetched)
        return totals + jnp.where((column < near_count)[:, None], contrib, 0.0)

    near_field = lax.fori_loop(
        0, jnp.max(near_count), near_step, jnp.zeros((tiles_dev, TILE), jnp.float32)
    )
    return near_field.reshape(pairs_dev) + far_field


def solution(mesh):
    return jax.shard_map(
        body,
        mesh=mesh,
        in_specs=(
            P(None, ("box", "pair")),
            P(("box", "pair")),
            P(None, ("box", "pair")),
            P(("box", "pair")),
            P(("box", "pair")),
            P(("box", "pair"), None),
            P(("box", "pair")),
            P("box", None),
            P("box", None),
            P(),
            P(),
            P(),
        ),
        out_specs=P(("box", "pair")),
        check_vma=False,
    )
```

profile of v0, /device:TPU:0, one launch (start us, length us, event | category | flops | bytes accessed | tf_op | source)
XLA Modules:
  0.0 283.2 jit_solution(612005292646290804)
XLA Ops:
  8.7 4.5 %collective-permute-start = (f32[5,2048]{1,0:T(8,128)S(1)}, f32[5,2048]{1,0:T(8,128)S(1)}, u32[]{:S(2)}, u32[]{:S(2)}) collective-permute-start(f32[5,2048]{1,0:T(8,128)S(1)} %pad_maximum_fusion.2), channel_id=1, source_target_pairs={{0,8},{8,16},{16,24},{24,32},{32,40},{40,48},{48,56},{56,64},{64,7... | collective-permute-start | bytes 122888 | tf_op jit(solution)/shard_map/ppermute | solution.py:20
  14.7 3.1 %fusion.57 = bf16[441,256]{1,0:T(8,128)(2,1)} fusion(bf16[441,2048]{1,0:T(8,128)(2,1)} %param.14, s32[2048]{0:T(1024)S(1)} %get-tuple-element.194, bf16[2048]{0:T(1024)(128)(2,1)S(1)} %convert_element_type.37), kind=kOutput, calls=%fused_computation.64 | convolution fusion | flops 463583488 | bytes 2044416 | tf_op jit(solution)/shard_map/dot_general | solution.py:86
  21.1 16.6 %all_gather.9 = f32[5,49152]{1,0:T(8,128)S(1)} all-gather(f32[5,6144]{1,0:T(8,128)S(1)} %pad_maximum_fusion.1), channel_id=1, replica_groups=mesh['box'=16,'pair'=8] {'pair'}, dimensions={1}, use_global_device_ids=true | all-gather | bytes 1105920 | tf_op jit(solution)/shard_map/all_gather | solution.py:79
  37.7 56.8 %while.13 = (s32[]{:T(128)}, f32[16,128]{1,0:T(8,128)S(1)}, s32[]{:T(128)}, s32[16]{0:T(128)S(1)}, f32[5,16,128]{2,1,0:T(8,128)S(1)}, /*index=5*/s32[16,24]{0,1:...) while((s32[]{:T(128)}, f32[16,128]{1,0:T(8,128)S(1)}, ...), condition=%wide.region_3.4_spmd, body=%wide.region_1.3_spmd.sunk | while | flops 4994869 | bytes 422435 | solution.py:144
  39.2 1.9 multiply_reduce_fusion.3
  63.8 1.9 multiply_reduce_fusion.3
  95.9 8.8 %collective-permute-start.2 = (bf16[441,2048]{1,0:T(8,128)(2,1)}, bf16[441,2048]{1,0:T(8,128)(2,1)}, u32[]{:S(2)}, u32[]{:S(2)}) collective-permute-start(bf16[441,2048]{1,0:T(8,128)(2,1)} %all-gather.2.cloned.1.call-done), channel_id=1, source_target_pairs={{0,8},{8,16},{16,24},{24,32},{32,40},{40,48},{48,56},{56,64},{64,7... | collective-permute-start | bytes 5419016 | tf_op jit(solution)/shard_map/ppermute | solution.py:20
  104.7 2.8 copy.35
  107.5 5.1 %fusion.58 = bf16[441,256]{1,0:T(8,128)(2,1)S(1)} fusion(bf16[8,441,441]{2,0,1:T(8,128)(2,1)} %param.23, bf16[441,256,8]{0,2,1:T(8,128)(2,1)S(1)} %bitcast.138), kind=kOutput, calls=%fused_computation.65 | convolution fusion | flops 796707072 | bytes 5143824 | tf_op jit(solution)/shard_map/opq,qmo->pm/dot_general | solution.py:98
  112.7 4.0 %fusion.75 = bf16[441,32]{0,1:T(8,128)(2,1)S(1)} fusion(bf16[8,441,441]{2,0,1:T(8,128)(2,1)} %param.23, bf16[441,32,8]{0,2,1:T(8,128)(2,1)S(1)} %bitcast.141), kind=kOutput, calls=%fused_computation.70 | convolution fusion | flops 99588384 | bytes 3365712 | tf_op jit(solution)/shard_map/opq,qmo->pm/dot_general | solution.py:98
  116.7 58.2 %all_gather.11 = bf16[441,512]{0,1:T(8,128)(2,1)S(1)} all-gather(bf16[441,32]{0,1:T(8,128)(2,1)S(1)} %fusion.75), channel_id=1, replica_groups=mesh['box'=16,'pair'=8] {'box'}, dimensions={1}, use_global_device_ids=true | all-gather | bytes 479808 | tf_op jit(solution)/shard_map/all_gather | solution.py:112
  174.9 2.1 gather_fusion.1
  177.0 13.7 %fusion.54 = bf16[441,32,8]{0,1,2:T(8,128)(2,1)S(1)} fusion(bf16[8,441,441]{2,0,1:T(8,128)(2,1)} %param.24, bf16[16,441,441]{2,0,1:T(8,128)(2,1)} %param.25, bf16[16,32,441]{2,1,0:T(8,128)(2,1)S(1)} %bitcast.136, pred[16,32]{1,0:T(8,128)(4,1)S(1)} %compare_bitcast_fusion.1, pred[16,32]{1,0:T(8,128)(4,1)S(1)} %broadcast_compare_fusion.1), kind=kOutput, calls=%fused_computation.63 | convolution fusion | flops 299301408 | bytes 10013488 | tf_op jit(solution)/shard_map/opq,qm->pmo/dot_general | solution.py:106
  190.7 6.4 %fusion.21 = f32[441,256,8]{1,0,2:T(8,128)} fusion(bf16[8,441,441]{2,0,1:T(8,128)(2,1)} %param.24, bf16[441,32,8]{0,1,2:T(8,128)(2,1)S(1)} %fusion.54), kind=kOutput, calls=%fused_computation.53 | convolution fusion | flops 796594176 | bytes 6950160 | tf_op jit(solution)/shard_map/opq,qm->pmo/dot_general | solution.py:106
  197.1 5.7 %copy.46 = f32[441,256,8]{0,2,1:T(8,128)} copy(f32[441,256,8]{1,0,2:T(8,128)} %fusion.21) | data formatting | bytes 7225344 | tf_op jit(solution)/shard_map/opq,qm->pmo/transpose | solution.py:106
  204.0 5.5 %pad_maximum_fusion = bf16[441,6144]{1,0:T(8,128)(2,1)} fusion(bf16[441,2048]{1,0:T(8,128)(2,1)} %collective-permute-done.3, bf16[441,2048]{1,0:T(8,128)(2,1)S(1)} %copy-done, bf16[441,2048]{1,0:T(8,128)(2,1)} %collective-permute-done.2), kind=kLoop, calls=%fused_computation.34 | loop fusion | flops 16257024 | bytes 10838016 | tf_op jit(solution)/shard_map/concatenate | solution.py:24
  209.5 8.3 %copy.48 = bf16[441,6144]{0,1:T(8,128)(2,1)} copy(bf16[441,6144]{1,0:T(8,128)(2,1)} %pad_maximum_fusion) | data formatting | bytes 10838016 | tf_op jit(solution)/shard_map/concatenate | solution.py:24
  217.8 21.0 %gather_fusion.2 = bf16[4096,441]{1,0:T(8,128)(2,1)} fusion(bf16[441,6144]{0,1:T(8,128)(2,1)} %copy.48, s32[4096]{0:T(1024)S(1)} %broadcast_clamp_fusion), kind=kCustom, calls=%fused_computation.2 | custom fusion | bytes 7241728 | tf_op jit(solution)/shard_map/jit(_take)/gather | solution.py:47
  238.8 6.2 %copy.49 = bf16[16,256,441]{1,2,0:T(8,128)(2,1)} copy(bf16[16,256,441]{2,1,0:T(8,128)(2,1)} %bitcast.135) | data formatting | bytes 7225344 | tf_op jit(solution)/shard_map/jit(_take)/gather | solution.py:47
  245.0 12.9 %fusion.49 = bf16[441,256]{1,0:T(8,128)(2,1)S(1)} fusion(f32[441,256]{1,0:T(8,128)S(1)} %copy.60, bf16[16,441,441]{2,0,1:T(8,128)(2,1)} %param.25, bf16[16,256,441]{1,2,0:T(8,128)(2,1)} %copy.49, pred[16,256]{1,0:T(8,128)(4,1)S(1)} %compare_bitcast_fusion, pred[16,256]{1,0:T(8,128)(4,1)S(1)} %compare_and_fusion), kind=kOutput, calls=%fused_computation.62 | convolution fusion | flops 1597026816 | bytes 10521632 | tf_op jit(solution)/shard_map/cpq,qct->pt/dot_general | solution.py:52
  258.0 7.5 %gather_fusion.3 = bf16[2048,441]{1,0:T(8,128)(2,1)S(1)} fusion(bf16[441,256]{0,1:T(8,128)(2,1)S(1)} %copy.51, s32[2048]{0:T(1024)S(1)} %fusion.105), kind=kCustom, calls=%fused_computation.3 | custom fusion | bytes 3620864 | tf_op jit(solution)/shard_map/jit(_take)/gather | solution.py:121
  265.6 2.2 select_convert_fusion
  267.8 5.5 %copy.58 = f32[2048,441]{0,1:T(8,128)} copy(f32[2048,441]{1,0:T(8,128)} %select_convert_fusion) | data formatting | bytes 7225344
  273.2 2.5 multiply_reduce_fusion.1
  (192 shorter events, 50.2 us)
Async XLA Ops:
  6.5 13.7 %copy-start.2 = (f32[3,2048]{1,0:T(4,128)S(1)}, f32[3,2048]{1,0:T(4,128)}, u32[]{:S(2)}) copy-start(f32[3,2048]{1,0:T(4,128)} %param.16) | copy-start | bytes 73732
  6.5 13.7 %copy-start.3 = (f32[2048]{0:T(1024)S(1)}, f32[2048]{0:T(1024)}, u32[]{:S(2)}) copy-start(f32[2048]{0:T(1024)} %param.15) | copy-start | bytes 24580
  6.5 13.7 %copy-start.4 = (f32[2048]{0:T(1024)S(1)}, f32[2048]{0:T(1024)}, u32[]{:S(2)}) copy-start(f32[2048]{0:T(1024)} %param.17) | copy-start | bytes 24580
  6.5 11.3 %copy-start.5 = (s32[32,16]{0,1:T(8,128)S(1)}, s32[32,16]{0,1:T(8,128)}, u32[]{:S(2)}) copy-start(s32[32,16]{0,1:T(8,128)} %param.22) | copy-start | bytes 6148
  6.5 13.8 %copy-start.6 = (s32[16,24]{1,0:T(8,128)S(1)}, s32[16,24]{1,0:T(8,128)}, u32[]{:S(2)}) copy-start(s32[16,24]{1,0:T(8,128)} %param.19) | copy-start | bytes 4612
  6.5 13.8 %copy-start.7 = (s32[16]{0:T(128)S(1)}, s32[16]{0:T(128)}, u32[]{:S(2)}) copy-start(s32[16]{0:T(128)} %param.20) | copy-start | bytes 196
  6.6 88.0 %all-gather.2.cloned.1.call-start = ((), (), s32[]{:S(2)}) async-start(), calls=%async_computation | async-start | bytes 2064384 | tf_op jit(solution)/shard_map/all_gather | solution.py:89
  7.4 13.6 %collective-permute-start.1 = (f32[5,2048]{1,0:T(8,128)S(1)}, f32[5,2048]{1,0:T(8,128)S(1)}, u32[]{:S(2)}, u32[]{:S(2)}) collective-permute-start(f32[5,2048]{1,0:T(8,128)S(1)} %pad_maximum_fusion.2), channel_id=1, source_target_pairs={{8,0},{16,8},{24,16},{32,24},{40,32},{48,40},{56,48},{64,56},{72,6... | collective-permute-start | bytes 122888 | tf_op jit(solution)/shard_map/ppermute | solution.py:23
  8.7 12.4 %collective-permute-start = (f32[5,2048]{1,0:T(8,128)S(1)}, f32[5,2048]{1,0:T(8,128)S(1)}, u32[]{:S(2)}, u32[]{:S(2)}) collective-permute-start(f32[5,2048]{1,0:T(8,128)S(1)} %pad_maximum_fusion.2), channel_id=1, source_target_pairs={{0,8},{8,16},{16,24},{24,32},{32,40},{40,48},{48,56},{56,64},{64,7... | collective-permute-start | bytes 122888 | tf_op jit(solution)/shard_map/ppermute | solution.py:20
  94.6 109.5 %collective-permute-start.3 = (bf16[441,2048]{1,0:T(8,128)(2,1)}, bf16[441,2048]{1,0:T(8,128)(2,1)}, u32[]{:S(2)}, u32[]{:S(2)}) collective-permute-start(bf16[441,2048]{1,0:T(8,128)(2,1)} %all-gather.2.cloned.1.call-done), channel_id=1, source_target_pairs={{8,0},{16,8},{24,16},{32,24},{40,32},{48,40},{56,48},{64,56},{72,6... | collective-permute-start | bytes 5419016 | tf_op jit(solution)/shard_map/ppermute | solution.py:23
  95.9 108.2 %collective-permute-start.2 = (bf16[441,2048]{1,0:T(8,128)(2,1)}, bf16[441,2048]{1,0:T(8,128)(2,1)}, u32[]{:S(2)}, u32[]{:S(2)}) collective-permute-start(bf16[441,2048]{1,0:T(8,128)(2,1)} %all-gather.2.cloned.1.call-done), channel_id=1, source_target_pairs={{0,8},{8,16},{16,24},{24,32},{32,40},{40,48},{48,56},{56,64},{64,7... | collective-permute-start | bytes 5419016 | tf_op jit(solution)/shard_map/ppermute | solution.py:20
  197.1 7.0 %copy-start = (bf16[441,2048]{1,0:T(8,128)(2,1)S(1)}, bf16[441,2048]{1,0:T(8,128)(2,1)}, u32[]{:S(2)}) copy-start(bf16[441,2048]{1,0:T(8,128)(2,1)} %all-gather.2.cloned.1.call-done) | copy-start | bytes 5419012
  267.8 5.5 %copy-start.1 = (bf16[441,2048]{1,0:T(8,128)(2,1)S(1)}, bf16[441,2048]{1,0:T(8,128)(2,1)}, u32[]{:S(2)}) copy-start(bf16[441,2048]{1,0:T(8,128)(2,1)} %param.14) | copy-start | bytes 5419012
Sparse Core Ops, SparseCore 0:
  18.0 31.3 all-gather.1
where the time goes:
time: 285 us; the launch traced here: 283 us
  blocking collectives  74.8 us (26%)
  local copies, waits for them, and re-layouts  70.5 us (25%)
  other arithmetic  50.2 us (18%)
  matrix products  45.1 us (16%)
  starting transfers between devices  16 us (6%)
  between operations  13.7 us (5%)
  loops' own time  13 us (5%)
    all_gather x1, blocking collectives, body(): all_coarse = lax.all_gather(coarse_moments, 'box', axis=1, tiled=True)  58.2 us
    reduce_sum x16, other arithmetic, interact(): return jnp.sum(reduced * shape_fn * source_tiles[4][:, None, :], axis=2)  30.9 us
    gather x3, local copies, waits for them, and re-layouts, gather_sources(): picked = jnp.take(table, columns, axis=1)  29.3 us
    dot_general x2, matrix products, descend(): jnp.einsum('opq,qm->pmo', l2l_ops, values, preferred_element_type=jnp.flo...  20 us
    all_gather x1, blocking collectives, body(): peer_data = lax.all_gather(rim_data, 'pair', axis=1, tiled=True)  16.6 us
    ppermute x2, starting transfers between devices, padded(): lax.ppermute(lax.slice_in_dim(block, block.shape[dim] - width, None, axis...  13.3 us
    another operation x1, loops' own time, body(): lax.fori_loop(0, jnp.max(near_count), near_step, jnp.zeros((tiles_dev, TI...  13 us
    dot_general x1, matrix products, translate(): jnp.einsum('cpq,qct->pt', operators, picked, preferred_element_type=jnp.f...  12.9 us
  transfers between devices with their start and end apart: 5, of which 0 were waited for; matrix products, arithmetic and copies ran while one was open for 33% of the time, Pallas kernels for 0%

commit v1 on v0

v1 whole, which is shorter than its diff:
```python
import jax
import jax.numpy as jnp
from jax import lax
from jax.experimental import pallas as pl
from jax.experimental.pallas import tpu as pltpu
from jax.sharding import PartitionSpec as P

MESH = pl.DeviceIdType.MESH
NT = (((1,), (1,)), ((), ()))
NN = (((1,), (0,)), ((), ()))
TILE = 128
TILES = 16
NNEAR = 24
COEF = 441
LEAF = 256
NCLASS = 16
BOXES = 16
LEAF_ROWS = 24 * LEAF
COARSE_ROWS = 512
ZERO_PAD = 16
f32, bf16 = jnp.float32, jnp.bfloat16

FIRST = [((0, 0), (0, 1)), ((0, 0), (0, 3)), ((0, 0), (1, 0)), ((0, 0), (-1, 0)), ((0, 0), (0, 2))]
SECOND = [((0, 3), (1, 0)), ((0, 3), (-1, 0)), ((0, 1), (1, 0)), ((0, 1), (-1, 0))]
THIRD_NEAR = [((-1, 3), (0, 1)), ((1, 1), (0, 3))]
THIRD_LEAF = [((-1, 3), (0, 1), 0), ((1, 3), (0, 1), 0), ((-1, 1), (0, 3), 1), ((1, 1), (0, 3), 1)]
ALL_SHARES = [(dx, dz) for dx in (-1, 0, 1) for dz in range(4)]


def split3(values):
    high = values.astype(bf16).astype(f32)
    rest = values - high
    middle = rest.astype(bf16).astype(f32)
    return high, middle, rest - middle


def kernel(
    near_tiles, near_count, coarse_source, mult_hbm, dens_ref, cent_ref, expo_ref, box_ref,
    m2l_source, m2m_hbm, l2l_hbm, m2l_hbm, out_ref,
    mult, m2m, l2l, m2l, idx_vmem, idx, near_tab, feat, leaf_tab, coarse_tab, sc3, onehot, rowidx,
    wide, tall, wd, spread, gat, acc, near_acc,
    loc_sem, near_send, near_recv, leaf_send, leaf_recv, coarse_send, coarse_recv,
):
    box = lax.axis_index("box")
    pair = lax.axis_index("pair")
    y, x = box // 4, box % 4
    z, core = pair // 2, pair % 2

    def slot_of(dx, dz, which):
        return (dx + 1) * 8 + ((z + dz) % 4) * 2 + which

    def near_device(ndx, ndz, flip=0):
        other = core if not flip else 1 - core
        return ((box + ndx + BOXES) % BOXES, ((z + ndz) % 4) * 2 + other)

    def plane_device(dy, dx, dz):
        return (((y + dy) % 4) * 4 + (x + dx) % 4, ((z + dz) % 4) * 2 + core)

    def local(i, src, dst):
        return pltpu.make_async_copy(src, dst, loc_sem.at[i])

    own_cols = pl.ds(pl.multiple_of(pair * LEAF, LEAF), LEAF)
    cp_mult = local(0, mult_hbm, mult)
    cp_m2m = local(1, m2m_hbm, m2m)
    cp_m2l = local(2, m2l_hbm, m2l)
    cp_l2l = local(3, l2l_hbm, l2l)
    cp_idx = local(4, m2l_source.at[:, own_cols], idx_vmem)
    cp_mult.start()
    cp_idx.start()
    cp_m2m.start()
    cp_m2l.start()
    cp_l2l.start()

    partners = [near_device(0, 1), near_device(0, 2), near_device(0, 3), near_device(1, 0)]
    partners += [near_device(-1, 0), near_device(0, 0, 1)]
    partners += [plane_device(0, d, 0) for d in (1, 2, 3)]
    partners += [plane_device(d, 0, 0) for d in (1, 2, 3)]
    barrier = pltpu.get_barrier_semaphore()
    for device in partners:
        pl.semaphore_signal(barrier, inc=1, device_id=device, device_id_type=MESH)

    own_slot = slot_of(0, 0, core)
    for c in range(3):
        for i in range(TILES):
            row = cent_ref[c : c + 1, i * TILE : (i + 1) * TILE] - 2.0
            near_tab[own_slot, c, i : i + 1, :] = row
    near_tab[own_slot, 3] = 1.0 / expo_ref[...]
    near_tab[own_slot, 4] = dens_ref[...]
    pl.semaphore_wait(barrier, len(partners))

    def near_ref(dx, dz, which):
        return near_tab.at[slot_of(dx, dz, which)]

    def leaf_ref(dx, dz, which, half=None):
        base, size = slot_of(dx, dz, which) * LEAF, LEAF
        if half is not None:
            base, size = base + half * (LEAF // 2), LEAF // 2
        return leaf_tab.at[pl.ds(base, size)]

    def near_copy(i, share, hop, flip=0):
        (dx, dz), (ndx, ndz) = share, hop
        return pltpu.make_async_remote_copy(
            src_ref=near_ref(dx, dz, core),
            dst_ref=near_tab.at[(dx - ndx + 1) * 8 + ((z + dz) % 4) * 2 + core],
            send_sem=near_send.at[i], recv_sem=near_recv.at[i],
            device_id=near_device(ndx, ndz, flip), device_id_type=MESH,
        )

    def leaf_copy(i, share, hop, half=None, flip=0):
        (dx, dz), (ndx, ndz) = share, hop
        return pltpu.make_async_remote_copy(
            src_ref=leaf_ref(dx, dz, core, half), dst_ref=leaf_ref(dx - ndx, dz, core, half),
            send_sem=leaf_send.at[i], recv_sem=leaf_recv.at[i],
            device_id=near_device(ndx, ndz, flip), device_id_type=MESH,
        )

    near_first = [near_copy(i, *t) for i, t in enumerate(FIRST)]
    near_second = [near_copy(5 + i, *t) for i, t in enumerate(SECOND)]
    near_third = [near_copy(9 + i, *t) for i, t in enumerate(THIRD_NEAR)]
    near_core = {s: near_copy(11 + i, s, (0, 0), 1) for i, s in enumerate(ALL_SHARES)}
    leaf_first = [leaf_copy(i, *t) for i, t in enumerate(FIRST)]
    leaf_second = [leaf_copy(5 + i, *t) for i, t in enumerate(SECOND)]
    leaf_third = [leaf_copy(9 + i, *t) for i, t in enumerate(THIRD_LEAF)]
    leaf_core = {s: leaf_copy(13 + i, s, (0, 0), None, 1) for i, s in enumerate(ALL_SHARES)}

    for cp in near_first:
        cp.start()
    near_core[(0, 0)].start()

    local_box = box_ref[...] - (box * (8 * LEAF) + pair * LEAF)
    rowidx[...] = (local_box % 8) * 32 + (local_box // 8 % 8) * 4 + local_box // 64
    row_iota = lax.broadcasted_iota(jnp.int32, (LEAF, TILE), 0)
    for i in range(TILES):
        weight = dens_ref[i : i + 1, :].astype(bf16).astype(f32)
        hit = row_iota == rowidx[i : i + 1, :]
        onehot[:, i * TILE : (i + 1) * TILE] = jnp.where(hit, weight, 0.0).astype(bf16)
    leaf_tab[pl.ds(LEAF_ROWS, ZERO_PAD)] = jnp.zeros((ZERO_PAD, 4, TILE), bf16)
    coarse_tab[pl.ds(COARSE_ROWS, ZERO_PAD)] = jnp.zeros((ZERO_PAD, 4, TILE), bf16)
    cp_mult.wait()
    leaf = lax.dot_general(onehot[...], mult[...], NT, preferred_element_type=f32)
    leaf = jnp.concatenate([leaf, jnp.zeros((LEAF, 512 - COEF), f32)], axis=1)
    for c in range(4):
        sc3[:, c, :] = leaf[:, c * TILE : (c + 1) * TILE]
    leaf_tab[pl.ds(own_slot * LEAF, LEAF)] = sc3[...].astype(bf16)
    for cp in leaf_first:
        cp.start()
    leaf_core[(0, 0)].start()

    def near_forward_second():
        near_first[0].wait_recv()
        near_second[0].start()
        near_second[1].start()
        near_core[(0, 3)].start()
        near_first[1].wait_recv()
        near_second[2].start()
        near_second[3].start()
        near_core[(0, 1)].start()
        near_first[2].wait_recv()
        near_core[(-1, 0)].start()
        near_first[3].wait_recv()
        near_core[(1, 0)].start()
        near_first[4].wait_recv()
        near_core[(0, 2)].start()

    def near_forward_third():
        near_second[0].wait_recv()
        near_third[0].start()
        near_core[(-1, 3)].start()
        near_second[3].wait_recv()
        near_third[1].start()
        near_core[(1, 1)].start()
        near_second[1].wait_recv()
        near_core[(1, 3)].start()
        near_second[2].wait_recv()
        near_core[(-1, 1)].start()

    def near_finish():
        near_third[0].wait_recv()
        near_core[(-1, 2)].start()
        near_third[1].wait_recv()
        near_core[(1, 2)].start()
        for cp in near_core.values():
            cp.wait_recv()

    def stream(operators, total, right, dims, columns):
        def chunk(start, size):
            rows = operators[pl.ds(start, size), :]
            result = lax.dot_general(rows, right, dims, preferred_element_type=f32)
            if columns == 256:
                wide[0, pl.ds(start, size), :] = result[:, :TILE]
                wide[1, pl.ds(start, size), :] = result[:, TILE:]
            else:
                tall[pl.ds(start, size), :] = result

        def step(i, carry):
            chunk(pl.multiple_of(i * 512, 512), 512)
            return carry

        whole = total // 512
        lax.fori_loop(0, whole, step, 0)
        if total % 512:
            chunk(whole * 512, total % 512)

    lane = lax.broadcasted_iota(jnp.int32, (COEF, TILE), 1)

    near_forward_second()

    cp_m2m.wait()
    stream(m2m, 8 * COEF, leaf[:, :COEF].astype(bf16), NT, 256)
    total = None
    for o in range(8):
        part = wide[o // 4, pl.ds(o, COEF, stride=8), :]
        part = jnp.where(lane // 32 == o % 4, part, 0.0)
        total = part if total is None else total + part
    total = total + pltpu.roll(total, 64, 1)
    total = total + pltpu.roll(total, 32, 1)
    near_forward_third()
    stream(m2m, 8 * COEF, total.astype(bf16), NN, 128)
    total = None
    for o in range(8):
        part = tall[pl.ds(o, COEF, stride=8), :]
        part = jnp.where(lane % 32 // 4 == o, part, 0.0)
        total = part if total is None else total + part
    for shift in (16, 8, 4):
        total = total + pltpu.roll(total, shift, 1)
    coarse = jnp.concatenate([total, jnp.zeros((512 - COEF, TILE), f32)], axis=0)
    coarse = jnp.transpose(coarse, (1, 0))
    for c in range(4):
        sc3[0:4, c, :] = coarse[0:4, c * TILE : (c + 1) * TILE]
    core_base, y_base, x_base = core * 256, y * 64, x * 16
    coarse_tab[pl.ds(core_base + y_base + x_base + z * 4, 4)] = sc3[0:4].astype(bf16)

    def coarse_copy(i, base, size, device):
        return pltpu.make_async_remote_copy(
            src_ref=coarse_tab.at[pl.ds(base, size)], dst_ref=coarse_tab.at[pl.ds(base, size)],
            send_sem=coarse_send.at[i], recv_sem=coarse_recv.at[i],
            device_id=device, device_id_type=MESH,
        )

    coarse_z = [
        coarse_copy(i, core_base + y_base + x_base + z * 4, 4, plane_device(0, 0, i + 1))
        for i in range(3)
    ]
    coarse_x = [
        coarse_copy(3 + i, core_base + y_base + x_base, 16, plane_device(0, i + 1, 0))
        for i in range(3)
    ]
    coarse_y = [
        coarse_copy(6 + i, core_base + y_base, 64, plane_device(i + 1, 0, 0)) for i in range(3)
    ]
    coarse_c = [coarse_copy(9, core_base, 256, near_device(0, 0, 1))]
    for cp in coarse_z:
        cp.start()

    near_finish()
    def features(s, carry):
        px, py, pz = near_tab[s, 0], near_tab[s, 1], near_tab[s, 2]
        rows = [px, py, pz, px * px + py * py + pz * pz, jnp.ones_like(px)]
        rows += [near_tab[s, 3], near_tab[s, 4], jnp.zeros_like(px)]
        for r, value in enumerate(rows):
            feat[pl.ds(s * TILES, TILES), r, :] = value
        return carry

    lax.fori_loop(0, 24, features, 0)

    def near_tile(u, carry):
        own = feat[own_slot * TILES + u]
        row = lax.broadcasted_iota(jnp.int32, (8, TILE), 0)
        left = jnp.where(row < 3, -2.0 * own, 0.0)
        left = jnp.where(row == 3, 1.0, left)
        left = jnp.where(row == 4, own[3:4, :], left)
        high, middle, low = split3(left)
        left = jnp.concatenate([high, middle, low, high, middle, high], axis=0)
        left = jnp.transpose(left, (1, 0)).astype(bf16)
        inverse = jnp.transpose(jnp.broadcast_to(own[5:6, :], (TILE, TILE)), (1, 0))
        count = near_count[u]

        def one(k):
            tile = near_tiles[u, k] - (box - 1) * (TILES * 8)
            tile = jnp.where(k < count, tile, 0)
            source = feat[tile]
            high, middle, low = split3(source)
            right = jnp.concatenate([high, high, high, middle, middle, low], axis=0).astype(bf16)
            square = lax.dot_general(left, right, NN, preferred_element_type=f32)
            square = jnp.maximum(square, 1e-9)
            weight = jnp.where(k < count, source[6:7, :], 0.0)
            scale = lax.rsqrt(inverse + source[5:6, :])
            reciprocal = lax.rsqrt(square)
            return lax.erf(square * reciprocal * scale) * (reciprocal * weight)

        def step(i, total):
            for j in range(4):
                total = total + one(i * 4 + j)
            return total

        total = lax.fori_loop(0, NNEAR // 4, step, jnp.zeros((TILE, TILE), f32))
        near_acc[pl.ds(u, 1), :] = jnp.transpose(jnp.sum(total, axis=1, keepdims=True), (1, 0))
        return carry


    cp_m2l.wait()
    spread[3] = jnp.zeros((1024, TILE), f32)

    def unmix(start, size):
        source = pl.ds(start * NCLASS, size * NCLASS)
        for c in range(4):
            width = min(TILE, COEF - c * TILE)
            rows = m2l[source, pl.ds(c * TILE, width)].astype(f32)
            spread[c, pl.ds(0, size * NCLASS), pl.ds(0, width)] = rows
        for k in range(NCLASS):
            for c in range(4):
                own = spread[c, pl.ds(k, size, stride=NCLASS), :]
                wd[k, pl.ds(start, size), pl.ds(c * TILE, TILE)] = own.astype(bf16)

    def unmix_step(i, carry):
        unmix(pl.multiple_of(i * 64, 64), 64)
        return carry

    lax.fori_loop(0, 6, unmix_step, 0)
    unmix(384, COEF - 384)

    cp_idx.wait()
    raw = idx_vmem[...]
    rel = jnp.clip(raw - (box - 1) * (8 * LEAF), 0, LEAF_ROWS - 1)
    row = (rel // LEAF) * LEAF + (rel % 8) * 32 + (rel // 8 % 8) * 4 + rel % LEAF // 64
    idx_vmem[...] = jnp.where(raw < 0, LEAF_ROWS, row)
    cp_smem = local(5, idx_vmem, idx)
    cp_smem.start()

    def near_tiles_of(first, last):
        lax.fori_loop(first, last, near_tile, 0)

    for cp in coarse_z:
        cp.wait_recv()
    for cp in coarse_x:
        cp.start()
    leaf_first[0].wait_recv()
    leaf_second[0].start()
    leaf_second[1].start()
    leaf_core[(0, 3)].start()
    leaf_first[1].wait_recv()
    leaf_second[2].start()
    leaf_second[3].start()
    leaf_core[(0, 1)].start()
    near_tiles_of(0, 4)
    for cp in coarse_x:
        cp.wait_recv()
    for cp in coarse_y:
        cp.start()
    leaf_first[2].wait_recv()
    leaf_core[(-1, 0)].start()
    leaf_first[3].wait_recv()
    leaf_core[(1, 0)].start()
    near_tiles_of(4, 8)
    for cp in coarse_y:
        cp.wait_recv()
    coarse_c[0].start()
    for i, share in enumerate([(-1, 3), (1, 3), (-1, 1), (1, 1)]):
        leaf_second[i].wait_recv()
        leaf_third[i].start()
        leaf_core[share].start()
    leaf_first[4].wait_recv()
    leaf_core[(0, 2)].start()
    near_tiles_of(8, 12)
    coarse_c[0].wait_recv()

    for k in range(NCLASS):
        for t in range(4):
            g = coarse_source[k, pair * 4 + t]
            home, member = g >> 5, (g >> 2) & 7
            place = (member & 1) * 256 + home * 16 + (member >> 1) * 4 + (g & 3)
            place = jnp.where(g < 0, COARSE_ROWS, place)
            gat[0, pl.ds((k * 4 + t) * 4, 4), :] = coarse_tab[place].astype(f32)
    picked = [gat[0, pl.ds(c, 64, stride=4), :] for c in range(4)]
    picked = jnp.concatenate(picked, axis=1)
    picked = jnp.concatenate([picked, picked], axis=0).astype(bf16)
    stream(m2l, NCLASS * COEF, picked[:, :COEF], NT, 128)
    total = None
    for k in range(NCLASS):
        part = tall[pl.ds(k, COEF, stride=NCLASS), :]
        part = jnp.where(lane % 64 // 4 == k, part, 0.0)
        total = part if total is None else total + part
    for shift in (32, 16, 8, 4):
        total = total + pltpu.roll(total, shift, 1)

    cp_l2l.wait()
    stream(l2l, 8 * COEF, total.astype(bf16), NN, 128)
    total = None
    for o in range(8):
        part = tall[pl.ds(o, COEF, stride=8), :]
        part = jnp.where(lane % 32 // 4 == o, part, 0.0)
        total = part if total is None else total + part
    stream(l2l, 8 * COEF, total.astype(bf16), NN, 128)
    acc[...] = jnp.zeros((448, LEAF), f32)
    for side in range(2):
        total = None
        for o in range(4):
            part = tall[pl.ds(side * 4 + o, COEF, stride=8), :]
            part = jnp.where(lane // 32 == o, part, 0.0)
            total = part if total is None else total + part
        acc[pl.ds(0, COEF), pl.ds(side * TILE, TILE)] = total

    leaf_third[0].wait_recv()
    leaf_third[2].wait_recv()
    leaf_core[(-1, 2)].start()
    leaf_third[1].wait_recv()
    leaf_third[3].wait_recv()
    leaf_core[(1, 2)].start()
    near_tiles_of(12, 16)
    cp_smem.wait()
    for cp in leaf_core.values():
        cp.wait_recv()

    def leaf_class(k, carry):
        slot = k % 2

        def rows(i, carry2):
            values = []
            for j in range(64):
                column = (j % 4) * 64 + (j % 32 // 4) * 8 + i * 2 + j // 32
                values.append(leaf_tab[idx[k, column]].astype(f32))
            base = pl.multiple_of(i * 256, 256)
            for j in range(64):
                gat[slot, pl.ds(base + j * 4, 4), :] = values[j]
            return carry2

        lax.fori_loop(0, 4, rows, 0)
        picked = [gat[slot, pl.ds(c, LEAF, stride=4), :].astype(bf16) for c in range(4)]
        picked = jnp.concatenate(picked, axis=1)
        acc[...] += lax.dot_general(wd[k], picked, NT, preferred_element_type=f32)
        return carry

    lax.fori_loop(0, NCLASS, leaf_class, 0)

    locals_ = jnp.transpose(acc[...], (1, 0)).astype(bf16)[:, :COEF]
    for q in range(8):
        columns = mult[:, q * 256 : (q + 1) * 256]
        product = lax.dot_general(locals_, columns, NN, preferred_element_type=f32)
        for h in range(2):
            i = q * 2 + h
            hit = row_iota == rowidx[i : i + 1, :]
            far = jnp.where(hit, product[:, h * TILE : (h + 1) * TILE], 0.0)
            far = jnp.sum(far, axis=0, keepdims=True)
            out_ref[i : i + 1, :] = near_acc[i : i + 1, :] + far

    copies = near_first + near_second + near_third + list(near_core.values())
    copies += leaf_first + leaf_second + leaf_third + list(leaf_core.values())
    copies += coarse_z + coarse_x + coarse_y + coarse_c
    for cp in copies:
        cp.wait_send()


def body(
    multipoles, density, pair_centers, pair_exponent, box_of_pair, near_tiles, near_count,
    m2l_source, coarse_source, m2m_ops, l2l_ops, m2l_ops,
):
    def flat(operators):
        return jnp.transpose(operators, (1, 0, 2)).reshape(-1, COEF)

    grid = (TILES, TILE)
    smem = pl.BlockSpec(memory_space=pltpu.SMEM)
    vmem = pl.BlockSpec(memory_space=pltpu.VMEM)
    anywhere = pl.BlockSpec(memory_space=pl.ANY)
    dma = pltpu.SemaphoreType.DMA
    out = pl.pallas_call(
        kernel,
        out_shape=jax.ShapeDtypeStruct(grid, f32),
        in_specs=[smem, smem, smem, anywhere, vmem, vmem, vmem, vmem]
        + [anywhere, anywhere, anywhere, anywhere],
        out_specs=vmem,
        scratch_shapes=[
            pltpu.VMEM((COEF, 2048), bf16),
            pltpu.VMEM((8 * COEF, COEF), bf16),
            pltpu.VMEM((8 * COEF, COEF), bf16),
            pltpu.VMEM((NCLASS * COEF, COEF), bf16),
            pltpu.VMEM((NCLASS, LEAF), jnp.int32),
            pltpu.SMEM((NCLASS, LEAF), jnp.int32),
            pltpu.VMEM((24, 5, TILES, TILE), f32),
            pltpu.VMEM((24 * TILES, 8, TILE), f32),
            pltpu.VMEM((LEAF_ROWS + ZERO_PAD, 4, TILE), bf16),
            pltpu.VMEM((COARSE_ROWS + ZERO_PAD, 4, TILE), bf16),
            pltpu.VMEM((LEAF, 4, TILE), f32),
            pltpu.VMEM((LEAF, 2048), bf16),
            pltpu.VMEM(grid, jnp.int32),
            pltpu.VMEM((2, 8 * COEF, TILE), f32),
            pltpu.VMEM((NCLASS * COEF, TILE), f32),
            pltpu.VMEM((NCLASS, 448, 512), bf16),
            pltpu.VMEM((4, 1024, TILE), f32),
            pltpu.VMEM((2, 1024, TILE), f32),
            pltpu.VMEM((448, LEAF), f32),
            pltpu.VMEM(grid, f32),
            dma((6,)),
            dma((23,)), dma((23,)), dma((25,)), dma((25,)), dma((10,)), dma((10,)),
        ],
        compiler_params=pltpu.CompilerParams(
            collective_id=0, has_side_effects=True, vmem_limit_bytes=60 * 1024 * 1024
        ),
    )(
        near_tiles, near_count, jnp.transpose(coarse_source), multipoles,
        density.reshape(grid), pair_centers, pair_exponent.reshape(grid),
        box_of_pair.reshape(grid), jnp.transpose(m2l_source),
        flat(m2m_ops), flat(l2l_ops), flat(m2l_ops),
    )
    return out.reshape(-1)


def solution(mesh):
    return jax.shard_map(
        body,
        mesh=mesh,
        in_specs=(
            P(None, ("box", "pair")),
            P(("box", "pair")),
            P(None, ("box", "pair")),
            P(("box", "pair")),
            P(("box", "pair")),
            P(("box", "pair"), None),
            P(("box", "pair")),
            P("box", None),
            P("box", None),
            P(),
            P(),
            P(),
        ),
        out_specs=P(("box", "pair")),
        check_vma=False,
    )
```

time: 285 us -> 97 us (0.34)
  the two profiles are of different devices: /device:TPU:0 before, /device:TPU:1 now
where the time goes in v1:
time: 97 us; the launch traced here: 96.8 us
  Pallas kernels  95.5 us (98%)
  local copies, waits for them, and re-layouts  1.3 us (1%)
    pallas_call x1, Pallas kernels, body(): pl.pallas_call(kernel, out_shape=jax.ShapeDtypeStruct(grid, f32), in_spec...  95.5 us

profile of v1, /device:TPU:1, one launch (start us, length us, event | category | flops | bytes accessed | tf_op | source)
XLA Modules:
  0.0 96.8 jit_solution(13967439691421528342)
XLA Ops:
  0.0 95.5 %shard_map.118 = f32[16,128]{1,0:T(8,128)} custom-call(s32[16,24]{1,0:T(8,128)} %near_tiles.1, s32[16]{0:T(128)} %near_count.1, s32[16,32]{1,0:T(8,128)} %bitcast.20, bf16[441,2048]{1,0:T(8,128)(2,1)} %mult_hbm.1, f32[16,128]{1,0:T(8,128)} %bitcast.21, f32[3,2048]{1,0:T(4,128)} %cent_ref.1, f32[16,128]{1,0:T(8,128)} %bitcast.22, s32[16,128]{1,0:T(8,128)} %bitcast.23, ...), custom_call_target="tpu_custom_call" | custom-call | tf_op jit(solution)/shard_map/pallas_call | solution.py:465
  95.5 1.3 %copy.14 = f32[2048]{0:T(1024)} copy(f32[2048]{0:T(1024)} %bitcast.19) | data formatting | bytes 16384

commit v2 on v1

--- a/solution.py
+++ b/solution.py
@@ -18,6 +18,7 @@
 LEAF_ROWS = 24 * LEAF
 COARSE_ROWS = 512
 ZERO_PAD = 16
+CHUNK = 1152
 f32, bf16 = jnp.float32, jnp.bfloat16
 
 FIRST = [((0, 0), (0, 1)), ((0, 0), (0, 3)), ((0, 0), (1, 0)), ((0, 0), (-1, 0)), ((0, 0), (0, 2))]
@@ -38,7 +39,7 @@
     near_tiles, near_count, coarse_source, mult_hbm, dens_ref, cent_ref, expo_ref, box_ref,
     m2l_source, m2m_hbm, l2l_hbm, m2l_hbm, out_ref,
     mult, m2m, l2l, m2l, idx_vmem, idx, near_tab, feat, leaf_tab, coarse_tab, sc3, onehot, rowidx,
-    wide, tall, wd, spread, gat, acc, near_acc,
+    wide, tall, wd, gat, gat_other, acc, near_acc,
     loc_sem, near_send, near_recv, leaf_send, leaf_recv, coarse_send, coarse_recv,
 ):
     box = lax.axis_index("box")
@@ -62,7 +63,7 @@
     own_cols = pl.ds(pl.multiple_of(pair * LEAF, LEAF), LEAF)
     cp_mult = local(0, mult_hbm, mult)
     cp_m2m = local(1, m2m_hbm, m2m)
-    cp_m2l = local(2, m2l_hbm, m2l)
+    cp_m2l = local(2, m2l_hbm, m2l.at[pl.ds(0, NCLASS * COEF)])
     cp_l2l = local(3, l2l_hbm, l2l)
     cp_idx = local(4, m2l_source.at[:, own_cols], idx_vmem)
     cp_mult.start()
@@ -142,9 +143,6 @@
     for c in range(4):
         sc3[:, c, :] = leaf[:, c * TILE : (c + 1) * TILE]
     leaf_tab[pl.ds(own_slot * LEAF, LEAF)] = sc3[...].astype(bf16)
-    for cp in leaf_first:
-        cp.start()
-    leaf_core[(0, 0)].start()
 
     def near_forward_second():
         near_first[0].wait_recv()
@@ -193,17 +191,20 @@
                 tall[pl.ds(start, size), :] = result
 
         def step(i, carry):
-            chunk(pl.multiple_of(i * 512, 512), 512)
+            chunk(pl.multiple_of(i * CHUNK, CHUNK), CHUNK)
             return carry
 
-        whole = total // 512
+        whole = total // CHUNK
         lax.fori_loop(0, whole, step, 0)
-        if total % 512:
-            chunk(whole * 512, total % 512)
+        if total % CHUNK:
+            chunk(whole * CHUNK, total % CHUNK)
 
     lane = lax.broadcasted_iota(jnp.int32, (COEF, TILE), 1)
 
     near_forward_second()
+    for cp in leaf_first[:4]:
+        cp.start()
+    leaf_core[(0, 0)].start()
 
     cp_m2m.wait()
     stream(m2m, 8 * COEF, leaf[:, :COEF].astype(bf16), NT, 256)
@@ -215,6 +216,7 @@
     total = total + pltpu.roll(total, 64, 1)
     total = total + pltpu.roll(total, 32, 1)
     near_forward_third()
+    leaf_first[4].start()
     stream(m2m, 8 * COEF, total.astype(bf16), NN, 128)
     total = None
     for o in range(8):
@@ -252,7 +254,6 @@
     for cp in coarse_z:
         cp.start()
 
-    near_finish()
     def features(s, carry):
         px, py, pz = near_tab[s, 0], near_tab[s, 1], near_tab[s, 2]
         rows = [px, py, pz, px * px + py * py + pz * pz, jnp.ones_like(px)]
@@ -261,7 +262,6 @@
             feat[pl.ds(s * TILES, TILES), r, :] = value
         return carry
 
-    lax.fori_loop(0, 24, features, 0)
 
     def near_tile(u, carry):
         own = feat[own_slot * TILES + u]
@@ -288,52 +288,61 @@
             reciprocal = lax.rsqrt(square)
             return lax.erf(square * reciprocal * scale) * (reciprocal * weight)
 
-        def step(i, total):
-            for j in range(4):
-                total = total + one(i * 4 + j)
-            return total
-
-        total = lax.fori_loop(0, NNEAR // 4, step, jnp.zeros((TILE, TILE), f32))
+        total = jnp.zeros((TILE, TILE), f32)
+        for k in range(NNEAR):
+            total = total + one(k)
         near_acc[pl.ds(u, 1), :] = jnp.transpose(jnp.sum(total, axis=1, keepdims=True), (1, 0))
         return carry
 
 
-    cp_m2l.wait()
-    spread[3] = jnp.zeros((1024, TILE), f32)
-
-    def unmix(start, size):
-        source = pl.ds(start * NCLASS, size * NCLASS)
-        for c in range(4):
-            width = min(TILE, COEF - c * TILE)
-            rows = m2l[source, pl.ds(c * TILE, width)].astype(f32)
-            spread[c, pl.ds(0, size * NCLASS), pl.ds(0, width)] = rows
-        for k in range(NCLASS):
-            for c in range(4):
-                own = spread[c, pl.ds(k, size, stride=NCLASS), :]
-                wd[k, pl.ds(start, size), pl.ds(c * TILE, TILE)] = own.astype(bf16)
-
-    def unmix_step(i, carry):
-        unmix(pl.multiple_of(i * 64, 64), 64)
+    def steps_between(u):
+        @pl.when(u == 1)
+        def _():
+            for cp in coarse_x:
+                cp.wait_recv()
+            for cp in coarse_y:
+                cp.start()
+
+        @pl.when(u == 3)
+        def _():
+            for i, share in enumerate([(-1, 3), (1, 3)]):
+                leaf_second[i].wait_recv()
+                leaf_third[i].start()
+                leaf_core[share].start()
+            leaf_first[2].wait_recv()
+            leaf_core[(-1, 0)].start()
+            leaf_first[3].wait_recv()
+            leaf_core[(1, 0)].start()
+
+        @pl.when(u == 4)
+        def _():
+            for cp in coarse_y:
+                cp.wait_recv()
+            coarse_c[0].start()
+
+        @pl.when(u == 8)
+        def _():
+            for i, share in enumerate([(-1, 1), (1, 1)]):
+                leaf_second[2 + i].wait_recv()
+                leaf_third[2 + i].start()
+                leaf_core[share].start()
+            leaf_first[4].wait_recv()
+            leaf_core[(0, 2)].start()
+
+        @pl.when(u == 12)
+        def _():
+            leaf_third[0].wait_recv()
+            leaf_third[2].wait_recv()
+            leaf_core[(-1, 2)].start()
+            leaf_third[1].wait_recv()
+            leaf_third[3].wait_recv()
+            leaf_core[(1, 2)].start()
+
+    def tile_and_steps(u, carry):
+        near_tile(u, carry)
+        steps_between(u)
         return carry
 
-    lax.fori_loop(0, 6, unmix_step, 0)
-    unmix(384, COEF - 384)
-
-    cp_idx.wait()
-    raw = idx_vmem[...]
-    rel = jnp.clip(raw - (box - 1) * (8 * LEAF), 0, LEAF_ROWS - 1)
-    row = (rel // LEAF) * LEAF + (rel % 8) * 32 + (rel // 8 % 8) * 4 + rel % LEAF // 64
-    idx_vmem[...] = jnp.where(raw < 0, LEAF_ROWS, row)
-    cp_smem = local(5, idx_vmem, idx)
-    cp_smem.start()
-
-    def near_tiles_of(first, last):
-        lax.fori_loop(first, last, near_tile, 0)
-
-    for cp in coarse_z:
-        cp.wait_recv()
-    for cp in coarse_x:
-        cp.start()
     leaf_first[0].wait_recv()
     leaf_second[0].start()
     leaf_second[1].start()
@@ -342,26 +351,41 @@
     leaf_second[2].start()
     leaf_second[3].start()
     leaf_core[(0, 1)].start()
-    near_tiles_of(0, 4)
+
+    cp_m2l.wait()
+    m2l[pl.ds(NCLASS * COEF, NCLASS * 7), :] = jnp.zeros((NCLASS * 7, COEF), bf16)
+    into = lax.broadcasted_iota(jnp.int32, (256, 256), 0)
+    outof = lax.broadcasted_iota(jnp.int32, (256, 256), 1)
+    permute = (outof == into % 16 * NCLASS + into // 16).astype(f32).astype(bf16)
+
+    def unmix_step(i, carry):
+        for j in range(4):
+            start = pl.multiple_of((i * 4 + j) * 16, 16)
+            rows = m2l[pl.ds(pl.multiple_of(start * NCLASS, 256), 256), :]
+            apart = lax.dot_general(permute, rows, NN, preferred_element_type=f32)
+            apart = jnp.concatenate([apart, jnp.zeros((256, 512 - COEF), f32)], axis=1)
+            apart = apart.astype(bf16)
+            for k in range(NCLASS):
+                wd[k, pl.ds(start, 16), :] = apart[k * 16 : (k + 1) * 16, :]
+        return carry
+
+    lax.fori_loop(0, 7, unmix_step, 0)
+
+    cp_idx.wait()
+    raw = idx_vmem[...]
+    rel = jnp.clip(raw - (box - 1) * (8 * LEAF), 0, LEAF_ROWS - 1)
+    row = (rel // LEAF) * LEAF + (rel % 8) * 32 + (rel // 8 % 8) * 4 + rel % LEAF // 64
+    idx_vmem[...] = jnp.where(raw < 0, LEAF_ROWS, row)
+    cp_smem = local(5, idx_vmem, idx)
+    cp_smem.start()
+
+    for cp in coarse_z:
+        cp.wait_recv()
     for cp in coarse_x:
-        cp.wait_recv()
-    for cp in coarse_y:
         cp.start()
-    leaf_first[2].wait_recv()
-    leaf_core[(-1, 0)].start()
-    leaf_first[3].wait_recv()
-    leaf_core[(1, 0)].start()
-    near_tiles_of(4, 8)
-    for cp in coarse_y:
-        cp.wait_recv()
-    coarse_c[0].start()
-    for i, share in enumerate([(-1, 3), (1, 3), (-1, 1), (1, 1)]):
-        leaf_second[i].wait_recv()
-        leaf_third[i].start()
-        leaf_core[share].start()
-    leaf_first[4].wait_recv()
-    leaf_core[(0, 2)].start()
-    near_tiles_of(8, 12)
+    near_finish()
+    lax.fori_loop(0, 24, features, 0)
+    lax.fori_loop(0, TILES, tile_and_steps, 0)
     coarse_c[0].wait_recv()
 
     for k in range(NCLASS):
@@ -370,8 +394,8 @@
             home, member = g >> 5, (g >> 2) & 7
             place = (member & 1) * 256 + home * 16 + (member >> 1) * 4 + (g & 3)
             place = jnp.where(g < 0, COARSE_ROWS, place)
-            gat[0, pl.ds((k * 4 + t) * 4, 4), :] = coarse_tab[place].astype(f32)
-    picked = [gat[0, pl.ds(c, 64, stride=4), :] for c in range(4)]
+            gat[pl.ds((k * 4 + t) * 4, 4), :] = coarse_tab[place].astype(f32)
+    picked = [gat[pl.ds(c, 64, stride=4), :] for c in range(4)]
     picked = jnp.concatenate(picked, axis=1)
     picked = jnp.concatenate([picked, picked], axis=0).astype(bf16)
     stream(m2l, NCLASS * COEF, picked[:, :COEF], NT, 128)
@@ -400,37 +424,34 @@
             total = part if total is None else total + part
         acc[pl.ds(0, COEF), pl.ds(side * TILE, TILE)] = total
 
-    leaf_third[0].wait_recv()
-    leaf_third[2].wait_recv()
-    leaf_core[(-1, 2)].start()
-    leaf_third[1].wait_recv()
-    leaf_third[3].wait_recv()
-    leaf_core[(1, 2)].start()
-    near_tiles_of(12, 16)
     cp_smem.wait()
     for cp in leaf_core.values():
         cp.wait_recv()
 
-    def leaf_class(k, carry):
-        slot = k % 2
-
-        def rows(i, carry2):
+    def gather(k, into_ref):
+        for start in range(0, LEAF, 16):
             values = []
-            for j in range(64):
-                column = (j % 4) * 64 + (j % 32 // 4) * 8 + i * 2 + j // 32
+            for j in range(start, start + 16):
+                column = (j % 4) * 64 + (j % 32 // 4) * 8 + j // 32
                 values.append(leaf_tab[idx[k, column]].astype(f32))
-            base = pl.multiple_of(i * 256, 256)
-            for j in range(64):
-                gat[slot, pl.ds(base + j * 4, 4), :] = values[j]
-            return carry2
-
-        lax.fori_loop(0, 4, rows, 0)
-        picked = [gat[slot, pl.ds(c, LEAF, stride=4), :].astype(bf16) for c in range(4)]
+            for j in range(16):
+                into_ref[pl.ds((start + j) * 4, 4), :] = values[j]
+
+    def apply(k, from_ref):
+        picked = [from_ref[pl.ds(c, LEAF, stride=4), :].astype(bf16) for c in range(4)]
         picked = jnp.concatenate(picked, axis=1)
         acc[...] += lax.dot_general(wd[k], picked, NT, preferred_element_type=f32)
+
+    gather(0, gat)
+
+    def leaf_class(i, carry):
+        gather(2 * i + 1, gat_other)
+        apply(2 * i, gat)
+        gather(lax.rem(2 * i + 2, NCLASS), gat)
+        apply(2 * i + 1, gat_other)
         return carry
 
-    lax.fori_loop(0, NCLASS, leaf_class, 0)
+    lax.fori_loop(0, NCLASS // 2, leaf_class, 0)
 
     locals_ = jnp.transpose(acc[...], (1, 0)).astype(bf16)[:, :COEF]
     for q in range(8):
@@ -472,7 +493,7 @@
             pltpu.VMEM((COEF, 2048), bf16),
             pltpu.VMEM((8 * COEF, COEF), bf16),
             pltpu.VMEM((8 * COEF, COEF), bf16),
-            pltpu.VMEM((NCLASS * COEF, COEF), bf16),
+            pltpu.VMEM((NCLASS * 448, COEF), bf16),
             pltpu.VMEM((NCLASS, LEAF), jnp.int32),
             pltpu.SMEM((NCLASS, LEAF), jnp.int32),
             pltpu.VMEM((24, 5, TILES, TILE), f32),
@@ -485,8 +506,8 @@
             pltpu.VMEM((2, 8 * COEF, TILE), f32),
             pltpu.VMEM((NCLASS * COEF, TILE), f32),
             pltpu.VMEM((NCLASS, 448, 512), bf16),
-            pltpu.VMEM((4, 1024, TILE), f32),
-            pltpu.VMEM((2, 1024, TILE), f32),
+            pltpu.VMEM((1024, TILE), f32),
+            pltpu.VMEM((1024, TILE), f32),
             pltpu.VMEM((448, LEAF), f32),
             pltpu.VMEM(grid, f32),
             dma((6,)),

time: 97 us -> 69 us (0.71)
  the two profiles are of different devices: /device:TPU:1 before, /device:TPU:0 now
where the time goes in v2:
time: 69 us; the launch traced here: 68.8 us
  Pallas kernels  67.5 us (98%)
  local copies, waits for them, and re-layouts  1.3 us (2%)
    pallas_call x1, Pallas kernels, body(): pl.pallas_call(kernel, out_shape=jax.ShapeDtypeStruct(grid, f32), in_spec...  67.5 us

profile of v2, /device:TPU:0, one launch (start us, length us, event | category | flops | bytes accessed | tf_op | source)
XLA Modules:
  0.0 68.8 jit_solution(3368819122878723349)
XLA Ops:
  0.0 67.5 %shard_map.118 = f32[16,128]{1,0:T(8,128)} custom-call(s32[16,24]{1,0:T(8,128)} %near_tiles.1, s32[16]{0:T(128)} %near_count.1, s32[16,32]{1,0:T(8,128)} %bitcast.20, bf16[441,2048]{1,0:T(8,128)(2,1)} %mult_hbm.1, f32[16,128]{1,0:T(8,128)} %bitcast.21, f32[3,2048]{1,0:T(4,128)} %cent_ref.1, f32[16,128]{1,0:T(8,128)} %bitcast.22, s32[16,128]{1,0:T(8,128)} %bitcast.23, ...), custom_call_target="tpu_custom_call" | custom-call | tf_op jit(solution)/shard_map/pallas_call | solution.py:486
  67.5 1.3 %copy.14 = f32[2048]{0:T(1024)} copy(f32[2048]{0:T(1024)} %bitcast.19) | data formatting | bytes 16384

commit v3 on v2

--- a/solution.py
+++ b/solution.py
@@ -18,13 +18,17 @@
 LEAF_ROWS = 24 * LEAF
 COARSE_ROWS = 512
 ZERO_PAD = 16
-CHUNK = 1152
+CHUNK = 1184
 f32, bf16 = jnp.float32, jnp.bfloat16
 
-FIRST = [((0, 0), (0, 1)), ((0, 0), (0, 3)), ((0, 0), (1, 0)), ((0, 0), (-1, 0)), ((0, 0), (0, 2))]
-SECOND = [((0, 3), (1, 0)), ((0, 3), (-1, 0)), ((0, 1), (1, 0)), ((0, 1), (-1, 0))]
-THIRD_NEAR = [((-1, 3), (0, 1)), ((1, 1), (0, 3))]
-THIRD_LEAF = [((-1, 3), (0, 1), 0), ((1, 3), (0, 1), 0), ((-1, 1), (0, 3), 1), ((1, 1), (0, 3), 1)]
+HOPS = [(0, 1), (0, 3), (1, 0), (-1, 0), (0, 2)]
+NEAR_SECOND = [((0, dz), (dx, 0)) for dz in (3, 1, 2) for dx in (1, -1)]
+OWN = (0, 0)
+FIRST = [(OWN, (0, 1), 0), (OWN, (0, 3), 1), (OWN, (1, 0), None), (OWN, (-1, 0), None)]
+FIRST_B = [(OWN, (0, 1), 1), (OWN, (0, 3), 0), (OWN, (0, 2), None)]
+SECOND = [((0, 3), (1, 0), 0), ((0, 3), (-1, 0), 0), ((0, 1), (1, 0), 1), ((0, 1), (-1, 0), 1)]
+SECOND_B = [((0, 3), (1, 0), 1), ((0, 3), (-1, 0), 1), ((0, 1), (1, 0), 0), ((0, 1), (-1, 0), 0)]
+THIRD = [((-1, 3), (0, 1), 0), ((1, 3), (0, 1), 0), ((-1, 1), (0, 3), 1), ((1, 1), (0, 3), 1)]
 ALL_SHARES = [(dx, dz) for dx in (-1, 0, 1) for dz in range(4)]
 
 
@@ -39,7 +43,7 @@
     near_tiles, near_count, coarse_source, mult_hbm, dens_ref, cent_ref, expo_ref, box_ref,
     m2l_source, m2m_hbm, l2l_hbm, m2l_hbm, out_ref,
     mult, m2m, l2l, m2l, idx_vmem, idx, near_tab, feat, leaf_tab, coarse_tab, sc3, onehot, rowidx,
-    wide, tall, wd, gat, gat_other, acc, near_acc,
+    wide, tall, wd, gat, gat_other, acc, near_acc, picked_ref,
     loc_sem, near_send, near_recv, leaf_send, leaf_recv, coarse_send, coarse_recv,
 ):
     box = lax.axis_index("box")
@@ -72,8 +76,7 @@
     cp_m2l.start()
     cp_l2l.start()
 
-    partners = [near_device(0, 1), near_device(0, 2), near_device(0, 3), near_device(1, 0)]
-    partners += [near_device(-1, 0), near_device(0, 0, 1)]
+    partners = [near_device(*hop) for hop in HOPS] + [near_device(0, 0, 1)]
     partners += [plane_device(0, d, 0) for d in (1, 2, 3)]
     partners += [plane_device(d, 0, 0) for d in (1, 2, 3)]
     barrier = pltpu.get_barrier_semaphore()
@@ -115,14 +118,15 @@
             device_id=near_device(ndx, ndz, flip), device_id_type=MESH,
         )
 
-    near_first = [near_copy(i, *t) for i, t in enumerate(FIRST)]
-    near_second = [near_copy(5 + i, *t) for i, t in enumerate(SECOND)]
-    near_third = [near_copy(9 + i, *t) for i, t in enumerate(THIRD_NEAR)]
-    near_core = {s: near_copy(11 + i, s, (0, 0), 1) for i, s in enumerate(ALL_SHARES)}
+    near_first = [near_copy(i, OWN, hop) for i, hop in enumerate(HOPS)]
+    near_second = [near_copy(5 + i, *t) for i, t in enumerate(NEAR_SECOND)]
+    near_core = {s: near_copy(11 + i, s, OWN, 1) for i, s in enumerate(ALL_SHARES)}
     leaf_first = [leaf_copy(i, *t) for i, t in enumerate(FIRST)]
-    leaf_second = [leaf_copy(5 + i, *t) for i, t in enumerate(SECOND)]
-    leaf_third = [leaf_copy(9 + i, *t) for i, t in enumerate(THIRD_LEAF)]
-    leaf_core = {s: leaf_copy(13 + i, s, (0, 0), None, 1) for i, s in enumerate(ALL_SHARES)}
+    leaf_first_b = [leaf_copy(4 + i, *t) for i, t in enumerate(FIRST_B)]
+    leaf_second = [leaf_copy(7 + i, *t) for i, t in enumerate(SECOND)]
+    leaf_second_b = [leaf_copy(11 + i, *t) for i, t in enumerate(SECOND_B)]
+    leaf_third = [leaf_copy(15 + i, *t) for i, t in enumerate(THIRD)]
+    leaf_core = {s: leaf_copy(19 + i, s, OWN, None, 1) for i, s in enumerate(ALL_SHARES)}
 
     for cp in near_first:
         cp.start()
@@ -144,70 +148,33 @@
         sc3[:, c, :] = leaf[:, c * TILE : (c + 1) * TILE]
     leaf_tab[pl.ds(own_slot * LEAF, LEAF)] = sc3[...].astype(bf16)
 
-    def near_forward_second():
-        near_first[0].wait_recv()
-        near_second[0].start()
-        near_second[1].start()
-        near_core[(0, 3)].start()
-        near_first[1].wait_recv()
-        near_second[2].start()
-        near_second[3].start()
-        near_core[(0, 1)].start()
-        near_first[2].wait_recv()
-        near_core[(-1, 0)].start()
-        near_first[3].wait_recv()
-        near_core[(1, 0)].start()
-        near_first[4].wait_recv()
-        near_core[(0, 2)].start()
-
-    def near_forward_third():
-        near_second[0].wait_recv()
-        near_third[0].start()
-        near_core[(-1, 3)].start()
-        near_second[3].wait_recv()
-        near_third[1].start()
-        near_core[(1, 1)].start()
-        near_second[1].wait_recv()
-        near_core[(1, 3)].start()
-        near_second[2].wait_recv()
-        near_core[(-1, 1)].start()
-
-    def near_finish():
-        near_third[0].wait_recv()
-        near_core[(-1, 2)].start()
-        near_third[1].wait_recv()
-        near_core[(1, 2)].start()
-        for cp in near_core.values():
-            cp.wait_recv()
-
-    def stream(operators, total, right, dims, columns):
-        def chunk(start, size):
-            rows = operators[pl.ds(start, size), :]
-            result = lax.dot_general(rows, right, dims, preferred_element_type=f32)
-            if columns == 256:
-                wide[0, pl.ds(start, size), :] = result[:, :TILE]
-                wide[1, pl.ds(start, size), :] = result[:, TILE:]
-            else:
-                tall[pl.ds(start, size), :] = result
-
+    def product(operators, start, size, right, dims):
+        rows = operators[pl.ds(start, size), :]
+        result = lax.dot_general(rows, right, dims, preferred_element_type=f32)
+        if result.shape[1] == 256:
+            wide[0, pl.ds(start, size), :] = result[:, :TILE]
+            wide[1, pl.ds(start, size), :] = result[:, TILE:]
+        else:
+            tall[pl.ds(start, size), :] = result
+
+    def stream(operators, total, right, dims):
         def step(i, carry):
-            chunk(pl.multiple_of(i * CHUNK, CHUNK), CHUNK)
+            product(operators, pl.multiple_of(i * CHUNK, CHUNK), CHUNK, right, dims)
             return carry
 
         whole = total // CHUNK
         lax.fori_loop(0, whole, step, 0)
         if total % CHUNK:
-            chunk(whole * CHUNK, total % CHUNK)
+            product(operators, whole * CHUNK, total % CHUNK, right, dims)
 
     lane = lax.broadcasted_iota(jnp.int32, (COEF, TILE), 1)
 
-    near_forward_second()
-    for cp in leaf_first[:4]:
-        cp.start()
+    leaf_first[0].start()
+    leaf_first[1].start()
     leaf_core[(0, 0)].start()
 
     cp_m2m.wait()
-    stream(m2m, 8 * COEF, leaf[:, :COEF].astype(bf16), NT, 256)
+    stream(m2m, 8 * COEF, leaf[:, :COEF].astype(bf16), NT)
     total = None
     for o in range(8):
         part = wide[o // 4, pl.ds(o, COEF, stride=8), :]
@@ -215,9 +182,14 @@
         total = part if total is None else total + part
     total = total + pltpu.roll(total, 64, 1)
     total = total + pltpu.roll(total, 32, 1)
-    near_forward_third()
-    leaf_first[4].start()
-    stream(m2m, 8 * COEF, total.astype(bf16), NN, 128)
+    for j, dz in enumerate((3, 1, 2)):
+        near_first[(0, 1, 4)[j]].wait_recv()
+        near_second[2 * j].start()
+        near_second[2 * j + 1].start()
+        near_core[(0, dz)].start()
+    leaf_first[2].start()
+    leaf_first[3].start()
+    stream(m2m, 8 * COEF, total.astype(bf16), NN)
     total = None
     for o in range(8):
         part = tall[pl.ds(o, COEF, stride=8), :]
@@ -253,6 +225,12 @@
     coarse_c = [coarse_copy(9, core_base, 256, near_device(0, 0, 1))]
     for cp in coarse_z:
         cp.start()
+    for cp in leaf_first_b:
+        cp.start()
+    near_first[2].wait_recv()
+    near_core[(-1, 0)].start()
+    near_first[3].wait_recv()
+    near_core[(1, 0)].start()
 
     def features(s, carry):
         px, py, pz = near_tab[s, 0], near_tab[s, 1], near_tab[s, 2]
@@ -298,59 +276,50 @@
     def steps_between(u):
         @pl.when(u == 1)
         def _():
+            leaf_first_b[0].wait_recv()
+            leaf_second_b[0].start()
+            leaf_second_b[1].start()
+            leaf_core[(0, 3)].start()
+            leaf_first_b[1].wait_recv()
+            leaf_second_b[2].start()
+            leaf_second_b[3].start()
+            leaf_core[(0, 1)].start()
+            leaf_first[2].wait_recv()
+            leaf_core[(-1, 0)].start()
+            leaf_first[3].wait_recv()
+            leaf_core[(1, 0)].start()
+
+        @pl.when(u == 4)
+        def _():
             for cp in coarse_x:
                 cp.wait_recv()
             for cp in coarse_y:
                 cp.start()
 
-        @pl.when(u == 3)
-        def _():
-            for i, share in enumerate([(-1, 3), (1, 3)]):
-                leaf_second[i].wait_recv()
-                leaf_third[i].start()
-                leaf_core[share].start()
-            leaf_first[2].wait_recv()
-            leaf_core[(-1, 0)].start()
-            leaf_first[3].wait_recv()
-            leaf_core[(1, 0)].start()
-
-        @pl.when(u == 4)
+        @pl.when(u == 6)
         def _():
             for cp in coarse_y:
                 cp.wait_recv()
             coarse_c[0].start()
 
-        @pl.when(u == 8)
+        @pl.when(u == 9)
         def _():
-            for i, share in enumerate([(-1, 1), (1, 1)]):
-                leaf_second[2 + i].wait_recv()
-                leaf_third[2 + i].start()
+            for i in range(4):
+                leaf_second[i].wait_recv()
+                leaf_third[i].start()
+            leaf_first_b[2].wait_recv()
+            leaf_core[(0, 2)].start()
+
+        @pl.when(u == 13)
+        def _():
+            for i, share in enumerate([(-1, 3), (1, 3), (-1, 1), (1, 1)]):
+                leaf_second_b[i].wait_recv()
                 leaf_core[share].start()
-            leaf_first[4].wait_recv()
-            leaf_core[(0, 2)].start()
-
-        @pl.when(u == 12)
-        def _():
-            leaf_third[0].wait_recv()
-            leaf_third[2].wait_recv()
-            leaf_core[(-1, 2)].start()
-            leaf_third[1].wait_recv()
-            leaf_third[3].wait_recv()
-            leaf_core[(1, 2)].start()
 
     def tile_and_steps(u, carry):
         near_tile(u, carry)
         steps_between(u)
         return carry
-
-    leaf_first[0].wait_recv()
-    leaf_second[0].start()
-    leaf_second[1].start()
-    leaf_core[(0, 3)].start()
-    leaf_first[1].wait_recv()
-    leaf_second[2].start()
-    leaf_second[3].start()
-    leaf_core[(0, 1)].start()
 
     cp_m2l.wait()
     m2l[pl.ds(NCLASS * COEF, NCLASS * 7), :] = jnp.zeros((NCLASS * 7, COEF), bf16)
@@ -383,9 +352,19 @@
         cp.wait_recv()
     for cp in coarse_x:
         cp.start()
-    near_finish()
+    leaf_first[0].wait_recv()
+    leaf_second[0].start()
+    leaf_second[1].start()
+    leaf_first[1].wait_recv()
+    leaf_second[2].start()
+    leaf_second[3].start()
+    for ((_, dz), (dx, _)), cp in zip(NEAR_SECOND, near_second):
+        cp.wait_recv()
+        near_core[(-dx, dz)].start()
+    for cp in near_core.values():
+        cp.wait_recv()
     lax.fori_loop(0, 24, features, 0)
-    lax.fori_loop(0, TILES, tile_and_steps, 0)
+    lax.fori_loop(0, 8, tile_and_steps, 0)
     coarse_c[0].wait_recv()
 
     for k in range(NCLASS):
@@ -398,7 +377,15 @@
     picked = [gat[pl.ds(c, 64, stride=4), :] for c in range(4)]
     picked = jnp.concatenate(picked, axis=1)
     picked = jnp.concatenate([picked, picked], axis=0).astype(bf16)
-    stream(m2l, NCLASS * COEF, picked[:, :COEF], NT, 128)
+    picked_ref[...] = picked
+
+    def tile_and_m2l(i, carry):
+        start = jnp.minimum(i * CHUNK, NCLASS * COEF - CHUNK)
+        start = pl.multiple_of(start, 16)
+        product(m2l, start, CHUNK, picked_ref[:, :COEF], NT)
+        return tile_and_steps(i + 8, carry)
+
+    lax.fori_loop(0, 6, tile_and_m2l, 0)
     total = None
     for k in range(NCLASS):
         part = tall[pl.ds(k, COEF, stride=NCLASS), :]
@@ -408,13 +395,25 @@
         total = total + pltpu.roll(total, shift, 1)
 
     cp_l2l.wait()
-    stream(l2l, 8 * COEF, total.astype(bf16), NN, 128)
+    right = total.astype(bf16)
+    for i, (start, size) in enumerate([(0, 1776), (1776, 8 * COEF - 1776)]):
+        product(l2l, start, size, right, NN)
+    near_tile(14, 0)
     total = None
     for o in range(8):
         part = tall[pl.ds(o, COEF, stride=8), :]
         part = jnp.where(lane % 32 // 4 == o, part, 0.0)
         total = part if total is None else total + part
-    stream(l2l, 8 * COEF, total.astype(bf16), NN, 128)
+    right = total.astype(bf16)
+    for i, (start, size) in enumerate([(0, 1776), (1776, 8 * COEF - 1776)]):
+        product(l2l, start, size, right, NN)
+    near_tile(15, 0)
+    leaf_third[0].wait_recv()
+    leaf_third[2].wait_recv()
+    leaf_core[(-1, 2)].start()
+    leaf_third[1].wait_recv()
+    leaf_third[3].wait_recv()
+    leaf_core[(1, 2)].start()
     acc[...] = jnp.zeros((448, LEAF), f32)
     for side in range(2):
         total = None
@@ -464,8 +463,9 @@
             far = jnp.sum(far, axis=0, keepdims=True)
             out_ref[i : i + 1, :] = near_acc[i : i + 1, :] + far
 
-    copies = near_first + near_second + near_third + list(near_core.values())
-    copies += leaf_first + leaf_second + leaf_third + list(leaf_core.values())
+    copies = near_first + near_second + list(near_core.values())
+    copies += leaf_first + leaf_first_b + leaf_second + leaf_second_b + leaf_third
+    copies += list(leaf_core.values())
     copies += coarse_z + coarse_x + coarse_y + coarse_c
     for cp in copies:
         cp.wait_send()
@@ -510,8 +510,9 @@
             pltpu.VMEM((1024, TILE), f32),
             pltpu.VMEM((448, LEAF), f32),
             pltpu.VMEM(grid, f32),
+            pltpu.VMEM((TILE, 512), bf16),
             dma((6,)),
-            dma((23,)), dma((23,)), dma((25,)), dma((25,)), dma((10,)), dma((10,)),
+            dma((23,)), dma((23,)), dma((31,)), dma((31,)), dma((10,)), dma((10,)),
         ],
         compiler_params=pltpu.CompilerParams(
             collective_id=0, has_side_effects=True, vmem_limit_bytes=60 * 1024 * 1024

time: 69 us -> 64.2 us (0.930)
  the two profiles are of different devices: /device:TPU:0 before, /device:TPU:1 now
where the time goes in v3:
time: 64.2 us; the launch traced here: 64 us
  Pallas kernels  62.7 us (98%)
  local copies, waits for them, and re-layouts  1.3 us (2%)
    pallas_call x1, Pallas kernels, body(): pl.pallas_call(kernel, out_shape=jax.ShapeDtypeStruct(grid, f32), in_spec...  62.7 us
    unnamed x1, local copies, waits for them, and re-layouts  1.3 us

profile of v3, /device:TPU:1, one launch (start us, length us, event | category | flops | bytes accessed | tf_op | source)
XLA Modules:
  0.0 64.0 jit_solution(13292217295294104241)
XLA Ops:
  0.0 62.7 %shard_map.118 = f32[16,128]{1,0:T(8,128)} custom-call(s32[16,24]{1,0:T(8,128)} %near_tiles.1, s32[16]{0:T(128)} %near_count.1, s32[16,32]{1,0:T(8,128)} %bitcast.20, bf16[441,2048]{1,0:T(8,128)(2,1)} %mult_hbm.1, f32[16,128]{1,0:T(8,128)} %bitcast.21, f32[3,2048]{1,0:T(4,128)} %cent_ref.1, f32[16,128]{1,0:T(8,128)} %bitcast.22, s32[16,128]{1,0:T(8,128)} %bitcast.23, ...), custom_call_target="tpu_custom_call" | custom-call | tf_op jit(solution)/shard_map/pallas_call | solution.py:486
  62.7 1.3 %copy.14 = f32[2048]{0:T(1024)} copy(f32[2048]{0:T(1024)} %bitcast.19) | data formatting | bytes 16384

commit v4 on v3

--- a/solution.py
+++ b/solution.py
@@ -24,8 +24,9 @@
 HOPS = [(0, 1), (0, 3), (1, 0), (-1, 0), (0, 2)]
 NEAR_SECOND = [((0, dz), (dx, 0)) for dz in (3, 1, 2) for dx in (1, -1)]
 OWN = (0, 0)
-FIRST = [(OWN, (0, 1), 0), (OWN, (0, 3), 1), (OWN, (1, 0), None), (OWN, (-1, 0), None)]
+FIRST = [(OWN, (0, 1), 0), (OWN, (0, 3), 1), (OWN, (1, 0), 0), (OWN, (-1, 0), 0)]
 FIRST_B = [(OWN, (0, 1), 1), (OWN, (0, 3), 0), (OWN, (0, 2), None)]
+FIRST_B += [(OWN, (1, 0), 1), (OWN, (-1, 0), 1)]
 SECOND = [((0, 3), (1, 0), 0), ((0, 3), (-1, 0), 0), ((0, 1), (1, 0), 1), ((0, 1), (-1, 0), 1)]
 SECOND_B = [((0, 3), (1, 0), 1), ((0, 3), (-1, 0), 1), ((0, 1), (1, 0), 0), ((0, 1), (-1, 0), 0)]
 THIRD = [((-1, 3), (0, 1), 0), ((1, 3), (0, 1), 0), ((-1, 1), (0, 3), 1), ((1, 1), (0, 3), 1)]
@@ -123,10 +124,10 @@
     near_core = {s: near_copy(11 + i, s, OWN, 1) for i, s in enumerate(ALL_SHARES)}
     leaf_first = [leaf_copy(i, *t) for i, t in enumerate(FIRST)]
     leaf_first_b = [leaf_copy(4 + i, *t) for i, t in enumerate(FIRST_B)]
-    leaf_second = [leaf_copy(7 + i, *t) for i, t in enumerate(SECOND)]
-    leaf_second_b = [leaf_copy(11 + i, *t) for i, t in enumerate(SECOND_B)]
-    leaf_third = [leaf_copy(15 + i, *t) for i, t in enumerate(THIRD)]
-    leaf_core = {s: leaf_copy(19 + i, s, OWN, None, 1) for i, s in enumerate(ALL_SHARES)}
+    leaf_second = [leaf_copy(9 + i, *t) for i, t in enumerate(SECOND)]
+    leaf_second_b = [leaf_copy(13 + i, *t) for i, t in enumerate(SECOND_B)]
+    leaf_third = [leaf_copy(17 + i, *t) for i, t in enumerate(THIRD)]
+    leaf_core = {s: leaf_copy(21 + i, s, OWN, None, 1) for i, s in enumerate(ALL_SHARES)}
 
     for cp in near_first:
         cp.start()
@@ -225,8 +226,8 @@
     coarse_c = [coarse_copy(9, core_base, 256, near_device(0, 0, 1))]
     for cp in coarse_z:
         cp.start()
-    for cp in leaf_first_b:
-        cp.start()
+    leaf_first_b[0].start()
+    leaf_first_b[1].start()
     near_first[2].wait_recv()
     near_core[(-1, 0)].start()
     near_first[3].wait_recv()
@@ -274,7 +275,7 @@
 
 
     def steps_between(u):
-        @pl.when(u == 1)
+        @pl.when(u == 3)
         def _():
             leaf_first_b[0].wait_recv()
             leaf_second_b[0].start()
@@ -284,10 +285,6 @@
             leaf_second_b[2].start()
             leaf_second_b[3].start()
             leaf_core[(0, 1)].start()
-            leaf_first[2].wait_recv()
-            leaf_core[(-1, 0)].start()
-            leaf_first[3].wait_recv()
-            leaf_core[(1, 0)].start()
 
         @pl.when(u == 4)
         def _():
@@ -296,25 +293,23 @@
             for cp in coarse_y:
                 cp.start()
 
-        @pl.when(u == 6)
+        @pl.when(u == 7)
         def _():
             for cp in coarse_y:
                 cp.wait_recv()
             coarse_c[0].start()
 
-        @pl.when(u == 9)
+        @pl.when(u == 11)
         def _():
+            for i, dx in enumerate((-1, 1)):
+                leaf_first[2 + i].wait_recv()
+                leaf_first_b[3 + i].wait_recv()
+                leaf_core[(dx, 0)].start()
             for i in range(4):
                 leaf_second[i].wait_recv()
                 leaf_third[i].start()
             leaf_first_b[2].wait_recv()
             leaf_core[(0, 2)].start()
-
-        @pl.when(u == 13)
-        def _():
-            for i, share in enumerate([(-1, 3), (1, 3), (-1, 1), (1, 1)]):
-                leaf_second_b[i].wait_recv()
-                leaf_core[share].start()
 
     def tile_and_steps(u, carry):
         near_tile(u, carry)
@@ -352,6 +347,9 @@
         cp.wait_recv()
     for cp in coarse_x:
         cp.start()
+    leaf_first_b[3].start()
+    leaf_first_b[4].start()
+    leaf_first_b[2].start()
     leaf_first[0].wait_recv()
     leaf_second[0].start()
     leaf_second[1].start()
@@ -364,7 +362,7 @@
     for cp in near_core.values():
         cp.wait_recv()
     lax.fori_loop(0, 24, features, 0)
-    lax.fori_loop(0, 8, tile_and_steps, 0)
+    lax.fori_loop(0, 10, tile_and_steps, 0)
     coarse_c[0].wait_recv()
 
     for k in range(NCLASS):
@@ -380,12 +378,12 @@
     picked_ref[...] = picked
 
     def tile_and_m2l(i, carry):
-        start = jnp.minimum(i * CHUNK, NCLASS * COEF - CHUNK)
+        start = jnp.minimum(i * 1776, NCLASS * COEF - 1776)
         start = pl.multiple_of(start, 16)
-        product(m2l, start, CHUNK, picked_ref[:, :COEF], NT)
-        return tile_and_steps(i + 8, carry)
-
-    lax.fori_loop(0, 6, tile_and_m2l, 0)
+        product(m2l, start, 1776, picked_ref[:, :COEF], NT)
+        return tile_and_steps(i + 10, carry)
+
+    lax.fori_loop(0, 4, tile_and_m2l, 0)
     total = None
     for k in range(NCLASS):
         part = tall[pl.ds(k, COEF, stride=NCLASS), :]
@@ -399,6 +397,9 @@
     for i, (start, size) in enumerate([(0, 1776), (1776, 8 * COEF - 1776)]):
         product(l2l, start, size, right, NN)
     near_tile(14, 0)
+    for i, share in enumerate([(-1, 3), (1, 3), (-1, 1), (1, 1)]):
+        leaf_second_b[i].wait_recv()
+        leaf_core[share].start()
     total = None
     for o in range(8):
         part = tall[pl.ds(o, COEF, stride=8), :]
@@ -512,7 +513,7 @@
             pltpu.VMEM(grid, f32),
             pltpu.VMEM((TILE, 512), bf16),
             dma((6,)),
-            dma((23,)), dma((23,)), dma((31,)), dma((31,)), dma((10,)), dma((10,)),
+            dma((23,)), dma((23,)), dma((33,)), dma((33,)), dma((10,)), dma((10,)),
         ],
         compiler_params=pltpu.CompilerParams(
             collective_id=0, has_side_effects=True, vmem_limit_bytes=60 * 1024 * 1024

time: 64.2 us -> 63.8 us (level)
  no operation moved by 1% of the time
where the time goes in v4:
time: 63.8 us; the launch traced here: 63.6 us
  Pallas kernels  62.3 us (98%)
  local copies, waits for them, and re-layouts  1.3 us (2%)
    pallas_call x1, Pallas kernels, body(): pl.pallas_call(kernel, out_shape=jax.ShapeDtypeStruct(grid, f32), in_spec...  62.3 us
    unnamed x1, local copies, waits for them, and re-layouts  1.3 us

profile of v4, /device:TPU:1, one launch (start us, length us, event | category | flops | bytes accessed | tf_op | source)
XLA Modules:
  0.0 63.6 jit_solution(6919969211927237202)
XLA Ops:
  0.0 62.3 %shard_map.118 = f32[16,128]{1,0:T(8,128)} custom-call(s32[16,24]{1,0:T(8,128)} %near_tiles.1, s32[16]{0:T(128)} %near_count.1, s32[16,32]{1,0:T(8,128)} %bitcast.20, bf16[441,2048]{1,0:T(8,128)(2,1)} %mult_hbm.1, f32[16,128]{1,0:T(8,128)} %bitcast.21, f32[3,2048]{1,0:T(4,128)} %cent_ref.1, f32[16,128]{1,0:T(8,128)} %bitcast.22, s32[16,128]{1,0:T(8,128)} %bitcast.23, ...), custom_call_target="tpu_custom_call" | custom-call | tf_op jit(solution)/shard_map/pallas_call | solution.py:487
  62.3 1.3 %copy.14 = f32[2048]{0:T(1024)} copy(f32[2048]{0:T(1024)} %bitcast.19) | data formatting | bytes 16384

commit v5 on v4

--- a/solution.py
+++ b/solution.py
@@ -362,7 +362,7 @@
     for cp in near_core.values():
         cp.wait_recv()
     lax.fori_loop(0, 24, features, 0)
-    lax.fori_loop(0, 10, tile_and_steps, 0)
+    lax.fori_loop(0, 12, tile_and_steps, 0)
     coarse_c[0].wait_recv()
 
     for k in range(NCLASS):
@@ -381,7 +381,7 @@
         start = jnp.minimum(i * 1776, NCLASS * COEF - 1776)
         start = pl.multiple_of(start, 16)
         product(m2l, start, 1776, picked_ref[:, :COEF], NT)
-        return tile_and_steps(i + 10, carry)
+        return tile_and_steps(i + 12, carry)
 
     lax.fori_loop(0, 4, tile_and_m2l, 0)
     total = None
@@ -396,7 +396,6 @@
     right = total.astype(bf16)
     for i, (start, size) in enumerate([(0, 1776), (1776, 8 * COEF - 1776)]):
         product(l2l, start, size, right, NN)
-    near_tile(14, 0)
     for i, share in enumerate([(-1, 3), (1, 3), (-1, 1), (1, 1)]):
         leaf_second_b[i].wait_recv()
         leaf_core[share].start()
@@ -408,7 +407,6 @@
     right = total.astype(bf16)
     for i, (start, size) in enumerate([(0, 1776), (1776, 8 * COEF - 1776)]):
         product(l2l, start, size, right, NN)
-    near_tile(15, 0)
     leaf_third[0].wait_recv()
     leaf_third[2].wait_recv()
     leaf_core[(-1, 2)].start()

time: 63.8 us -> 64.7 us (1.014)
  Pallas kernels: 62.3 us -> 63.2 us
    pallas_call x1, Pallas kernels: 62.3 us -> 63.2 us  [body(): pl.pallas_call(kernel, out_shape=jax.ShapeDtypeStruct(grid, f32), in_spec...]
where the time goes in v5:
time: 64.7 us; the launch traced here: 64.5 us
  Pallas kernels  63.2 us (98%)
  local copies, waits for them, and re-layouts  1.3 us (2%)
    pallas_call x1, Pallas kernels, body(): pl.pallas_call(kernel, out_shape=jax.ShapeDtypeStruct(grid, f32), in_spec...  63.2 us
    unnamed x1, local copies, waits for them, and re-layouts  1.3 us

profile of v5, /device:TPU:1, one launch (start us, length us, event | category | flops | bytes accessed | tf_op | source)
XLA Modules:
  0.0 64.5 jit_solution(1047649175547093186)
XLA Ops:
  0.0 63.2 %shard_map.118 = f32[16,128]{1,0:T(8,128)} custom-call(s32[16,24]{1,0:T(8,128)} %near_tiles.1, s32[16]{0:T(128)} %near_count.1, s32[16,32]{1,0:T(8,128)} %bitcast.20, bf16[441,2048]{1,0:T(8,128)(2,1)} %mult_hbm.1, f32[16,128]{1,0:T(8,128)} %bitcast.21, f32[3,2048]{1,0:T(4,128)} %cent_ref.1, f32[16,128]{1,0:T(8,128)} %bitcast.22, s32[16,128]{1,0:T(8,128)} %bitcast.23, ...), custom_call_target="tpu_custom_call" | custom-call | tf_op jit(solution)/shard_map/pallas_call | solution.py:485
  63.2 1.3 %copy.14 = f32[2048]{0:T(1024)} copy(f32[2048]{0:T(1024)} %bitcast.19) | data formatting | bytes 16384
